TPU v7x, 512 devices: a whole 4x4x16 slice. The times are simulated.
512 devices in a mesh: modes: 16 (over y, x_lo, core), sites: 32 (over x_hi, z).
Axes of the slice: x: 4 (x_hi: 2, x_lo: 2; x = x_hi * 2 + x_lo), y: 4, z: 16, core: 2. Of those that a mesh axis runs over, the one named last changes fastest.
Arguments:
- wave_state: float32 [4, 128, 131072], P(None, 'modes', 'sites'), may hold values from -6 to 6
- potential: float32 [131072], P('sites'), may hold values from -0.5 to 0.5
- spin_angle: float32 [131072], P('sites'), may hold values from -3.140625 to 3.140625
- magnet: float32 [3, 131072], P(None, 'sites'), may hold values from -0.6 to 0.6
- magnetic_mask: int32 [131072], P('sites'), may hold values 0 or 1
- mode_weight: float32 [128], P('modes'), may hold values from 0.5 to 2
- source_amp: float32 [4, 128], P(None, 'modes'), may hold values from -6 to 6
- mode_group: int32 [128], P('modes'), may hold values from 0 to 7
- energies: float32 [8], replicated, may hold values from -2 to 2
- lead_site: int32 [128], P('modes'), may hold values from 0 to 131071
Outputs:
- next_state: float32 [4, 128, 131072], P(None, 'modes', 'sites')
- densities: float32 [5, 131072], P(None, 'sites')
- magnet_next: float32 [3, 131072], P(None, 'sites')
All inputs are finite; a program needn't handle non-finite values. No bound on the sum of `magnetic_mask` on one device may be relied on, other than what follows from the above.
Results may differ from a plain program's by a relative error of at most 0.0001.
Values sent between devices are 32-bit elements; how exact they have to be, the bound alone decides.
A program may use at most 64 MiB of HBM per device.

v0:
```python
import math
import jax
import jax.numpy as jnp
from jax import lax
from jax.sharding import PartitionSpec as P

time_step = 0.6
start_time = 10.0
exchange_coupling = 0.5


def extended(cells, sides, width):
    for axis, dim in sides:
        count = lax.axis_size(axis)
        ends = count - 1
        head = lax.slice_in_dim(cells, 0, width, axis=dim)
        tail = lax.slice_in_dim(cells, cells.shape[dim] - width, cells.shape[dim], axis=dim)
        cells = jnp.concatenate(
            [
                lax.ppermute(tail, axis, [(i, (i + 1) % count) for i in range(ends)]),
                cells,
                lax.ppermute(head, axis, [((i + 1) % count, i) for i in range(ends)]),
            ],
            axis=dim,
        )
    return cells


def rotate_back(spinor, cosine, sine_term):
    shaped = spinor.reshape((2, 2) + spinor.shape[1:])
    spin_up = shaped[:, 0]
    spin_down = shaped[:, 1]
    turned = jnp.stack(
        [cosine * spin_up + sine_term * spin_down, cosine * spin_down - sine_term * spin_up], axis=1
    )
    return turned.reshape(spinor.shape)


def rotate_fore(spinor, cosine, sine_term):
    shaped = spinor.reshape((2, 2) + spinor.shape[1:])
    spin_up = shaped[:, 0]
    spin_down = shaped[:, 1]
    turned = jnp.stack(
        [cosine * spin_up - sine_term * spin_down, sine_term * spin_up + cosine * spin_down], axis=1
    )
    return turned.reshape(spinor.shape)


def exchange_term(spinor, sd_field):
    up_real, down_real, up_imag, down_imag = (spinor[0], spinor[1], spinor[2], spinor[3])
    field_x, field_y, field_z = (sd_field[0], sd_field[1], sd_field[2])
    out_up_real = field_z * up_real + field_x * down_real + field_y * down_imag
    out_down_real = field_x * up_real - field_y * up_imag - field_z * down_real
    out_up_imag = field_z * up_imag + field_x * down_imag - field_y * down_real
    out_down_imag = field_x * up_imag + field_y * up_real - field_z * down_imag
    return jnp.stack([out_up_real, out_down_real, out_up_imag, out_down_imag])


def source_field(offset, amplitude, energy, region):
    phase_angle = energy * (start_time + offset)
    cosine_phase = jnp.cos(phase_angle)
    sine_phase = jnp.sin(phase_angle)
    amp_real = amplitude[0:2]
    amp_imag = amplitude[2:4]
    real_part = amp_real * cosine_phase + amp_imag * sine_phase
    imag_part = amp_imag * cosine_phase - amp_real * sine_phase
    joined = jnp.concatenate([real_part, imag_part], axis=0)
    return joined[:, :, None] * region[None]


def rate(spinor, left_w, right_w, cosine, sine_term, potential, sd_field, source):
    hamil_term = (
        potential * spinor
        + exchange_term(spinor, sd_field)
        - rotate_fore(left_w + right_w, cosine, sine_term)
        + source
    )
    return jnp.concatenate([hamil_term[2:], -hamil_term[:2]], axis=0)


def densities_of(spinor, right_w, cosine, sine_term, weight_vec):
    up_real, down_real, up_imag, down_imag = (spinor[0], spinor[1], spinor[2], spinor[3])
    hopped = rotate_fore(right_w, cosine, sine_term)
    charge = up_real * up_real + down_real * down_real + up_imag * up_imag + down_imag * down_imag
    spin_x = 2.0 * (up_real * down_real + up_imag * down_imag)
    spin_y = 2.0 * (up_real * down_imag - up_imag * down_real)
    spin_z = up_real * up_real + up_imag * up_imag - down_real * down_real - down_imag * down_imag
    current = 2.0 * (
        up_real * hopped[2] + down_real * hopped[3] - up_imag * hopped[0] - down_imag * hopped[1]
    )
    stacked = jnp.stack([charge, spin_x, spin_y, spin_z, current])
    return jnp.sum(stacked * weight_vec[None, :, None], axis=1)


def advance(magnet, mask_float, totals):
    field_h = exchange_coupling * totals[1:4]
    torque = jnp.stack(
        [
            magnet[1] * field_h[2] - magnet[2] * field_h[1],
            magnet[2] * field_h[0] - magnet[0] * field_h[2],
            magnet[0] * field_h[1] - magnet[1] * field_h[0],
        ]
    )
    return magnet - time_step * (mask_float * torque)


def source_region(positions, lead_site, region_span):
    return (
        (positions[None, :] >= lead_site[:, None])
        & (positions[None, :] < lead_site[:, None] + region_span)
    ).astype(jnp.float32)


def local(
    wave_state,
    potential,
    spin_angle,
    magnet,
    magnetic_mask,
    mode_weight,
    source_amp,
    mode_group,
    energies,
    lead_site,
):
    local_sites = wave_state.shape[2]
    local_modes = wave_state.shape[1]
    site_count = lax.axis_size("sites")
    mode_count = lax.axis_size("modes")
    first_site = lax.axis_index("sites") * local_sites
    wire_sites = local_sites * site_count
    region_span = wire_sites // 8
    all_modes = local_modes * mode_count
    mask_float = magnetic_mask.astype(jnp.float32)
    group_ids = jnp.arange(energies.shape[0], dtype=jnp.int32)
    mode_energy = jnp.sum(
        jnp.where(
            mode_group[:, None] == group_ids[None, :],
            energies[None, :],
            jnp.zeros_like(energies)[None, :],
        ),
        axis=1,
    )
    cosine = jnp.cos(spin_angle)
    sine_term = jnp.sin(spin_angle)
    positions = first_site + jnp.arange(local_sites, dtype=jnp.int32)
    region = source_region(positions, lead_site, region_span)
    sd_field = exchange_coupling * mask_float * magnet

    def slope(spin_state, offset):
        weighted = rotate_back(spin_state, cosine, sine_term)
        padded = extended(weighted, (("sites", 2),), 1)
        source = source_field(offset, source_amp, mode_energy, region)
        return (
            rate(
                spin_state,
                padded[..., :-2],
                padded[..., 2:],
                cosine,
                sine_term,
                potential,
                sd_field,
                source,
            ),
            padded,
        )

    slope_one, padded_one = slope(wave_state, 0.0)
    slope_two, ignored = slope(wave_state + 0.5 * time_step * slope_one, 0.5 * time_step)
    slope_three, ignored = slope(wave_state + 0.5 * time_step * slope_two, 0.5 * time_step)
    slope_four, ignored = slope(wave_state + time_step * slope_three, time_step)
    next_state = wave_state + time_step / 6.0 * (
        slope_one + 2.0 * slope_two + 2.0 * slope_three + slope_four
    )
    right_w = padded_one[..., 2:]
    root_scale = 1.0 / math.sqrt(all_modes)
    row_scale = jnp.array(
        [1.0 / all_modes, root_scale, root_scale, root_scale, root_scale], jnp.float32
    )
    partial_value = (
        densities_of(wave_state, right_w, cosine, sine_term, mode_weight) * row_scale[:, None]
    )
    totals = lax.psum(partial_value, "modes")
    magnet_next = advance(magnet, mask_float, totals)
    return (next_state, totals, magnet_next)


def solution(mesh):
    return jax.shard_map(
        local,
        mesh=mesh,
        in_specs=(
            P(None, "modes", "sites"),
            P("sites"),
            P("sites"),
            P(None, "sites"),
            P("sites"),
            P("modes"),
            P(None, "modes"),
            P("modes"),
            P(),
            P("modes"),
        ),
        out_specs=(P(None, "modes", "sites"), P(None, "sites"), P(None, "sites")),
        check_vma=False,
    )
```

profile of v0, /device:TPU:1, one launch (start us, length us, event | category | flops | bytes accessed | tf_op | source)
XLA Modules:
  0.0 178.2 jit_solution(14860616858366607334)
XLA Ops:
  7.2 0.8 fusion.28
  8.0 1.1 multiply_add_fusion.13
  9.2 0.1 fusion.26
  9.2 4.5 %collective-permute-start = (f32[4,8,1]{2,1,0:T(8,128)S(1)}, f32[4,8,1]{2,1,0:T(8,128)S(1)}, u32[]{:S(2)}, u32[]{:S(2)}) collective-permute-start(f32[4,8,1]{2,1,0:T(8,128)S(1)} %get-tuple-element.55), channel_id=1, source_target_pairs={{0,1},{1,2},{2,3},{3,4},{4,5},{5,6},{6,7},{7,8},{8,9},{9,10},{10,1... | collective-permute-start | bytes 392 | tf_op jit(solution)/shard_map/ppermute | solution.py:20
  13.7 1.3 collective-permute-start.1
  15.2 0.1 multiply_add_fusion.17
  15.4 0.6 copy-done.13
  16.0 0.2 select_reduce_fusion
  16.2 0.1 multiply_cosine_fusion
  16.3 0.6 copy-done.10
  17.0 0.1 and_convert_fusion
  17.1 0.7 copy-done.9
  17.7 0.6 pad_maximum_fusion.20
  18.3 0.6 pad_maximum_fusion.22
  18.9 0.6 convert_element_type.10
  19.5 0.3 pad_maximum_fusion.6
  19.9 0.1 multiply_subtract_fusion
  20.0 0.1 pad_maximum_fusion.9
  20.1 0.6 copy-done.3
  20.7 0.1 fusion.5
  20.9 0.1 multiply_add_fusion.4
  21.0 0.1 multiply_add_fusion.16
  21.1 0.1 multiply_add_fusion.11
  21.2 0.7 fusion.24
  21.9 4.8 %collective-permute-start.2 = (f32[4,8,1]{2,1,0:T(8,128)}, f32[4,8,1]{2,1,0:T(8,128)}, u32[]{:S(2)}, u32[]{:S(2)}) collective-permute-start(f32[4,8,1]{2,1,0:T(8,128)} %get-tuple-element.50), channel_id=1, source_target_pairs={{0,1},{1,2},{2,3},{3,4},{4,5},{5,6},{6,7},{7,8},{8,9},{9,10},{10,1... | collective-permute-start | bytes 392 | tf_op jit(solution)/shard_map/ppermute | solution.py:20
  26.6 1.3 collective-permute-start.3
  27.9 0.1 fusion.14
  28.0 0.6 copy-done.12
  28.6 0.3 multiply_reduce_fusion
  28.8 0.4 copy-done.11
  29.2 0.7 broadcast_multiply_fusion
  30.0 1.4 collective-permute-done.3
  31.4 1.1 fusion.2
  32.5 0.1 multiply_subtract_fusion.5
  32.6 0.7 copy-done.4
  33.3 0.1 multiply_add_fusion.1
  33.5 0.1 multiply_add_fusion.3
  33.6 0.1 multiply_add_fusion.9
  33.7 0.1 fusion.22
  33.7 4.4 %collective-permute-start.4 = (f32[4,8,1]{2,1,0:T(8,128)S(1)}, f32[4,8,1]{2,1,0:T(8,128)S(1)}, u32[]{:S(2)}, u32[]{:S(2)}) collective-permute-start(f32[4,8,1]{2,1,0:T(8,128)S(1)} %get-tuple-element.46), channel_id=1, source_target_pairs={{0,1},{1,2},{2,3},{3,4},{4,5},{5,6},{6,7},{7,8},{8,9},{9,10},{10,1... | collective-permute-start | bytes 392 | tf_op jit(solution)/shard_map/ppermute | solution.py:20
  38.1 1.3 collective-permute-start.5
  39.4 0.1 multiply_add_fusion.15
  39.5 4.3 %collective-permute-done.5 = f32[4,8,1]{2,1,0:T(8,128)S(1)} collective-permute-done((f32[4,8,1]{2,1,0:T(8,128)S(1)}, f32[4,8,1]{2,1,0:T(8,128)S(1)}, u32[]{:S(2)}, u32[]{:S(2)}) %collective-permute-start.5) | collective-permute-done | bytes 160 | tf_op jit(solution)/shard_map/ppermute | solution.py:22
  43.8 0.3 fusion.1
  44.1 0.1 multiply_subtract_fusion.3
  44.3 0.1 multiply_add_fusion
  44.4 0.1 multiply_add_fusion.2
  44.5 0.1 multiply_add_fusion.7
  44.6 0.1 fusion.20
  44.7 4.6 %collective-permute-start.6 = (f32[4,8,1]{2,1,0:T(8,128)S(1)}, f32[4,8,1]{2,1,0:T(8,128)S(1)}, u32[]{:S(2)}, u32[]{:S(2)}) collective-permute-start(f32[4,8,1]{2,1,0:T(8,128)S(1)} %get-tuple-element.42), channel_id=1, source_target_pairs={{0,1},{1,2},{2,3},{3,4},{4,5},{5,6},{6,7},{7,8},{8,9},{9,10},{10,1... | collective-permute-start | bytes 392 | tf_op jit(solution)/shard_map/ppermute | solution.py:20
  49.3 1.3 collective-permute-start.7
  50.6 0.1 multiply_add_fusion.14
  50.7 3.1 %collective-permute-done.7 = f32[4,8,1]{2,1,0:T(8,128)S(1)} collective-permute-done((f32[4,8,1]{2,1,0:T(8,128)S(1)}, f32[4,8,1]{2,1,0:T(8,128)S(1)}, u32[]{:S(2)}, u32[]{:S(2)}) %collective-permute-start.7) | collective-permute-done | bytes 160 | tf_op jit(solution)/shard_map/ppermute | solution.py:22
  53.8 0.3 fusion
  54.1 0.1 multiply_subtract_fusion.1
  54.2 0.7 copy-done.8
  54.9 0.1 fusion.9
  55.1 1.0 fusion.11
  56.1 112.7 %all-reduce.2.cloned.1.call-done = f32[5,4096]{1,0:T(8,128)} async-done(((f32[5,4096]{1,0:T(8,128)}), f32[5,4096]{1,0:T(8,128)}) %all-reduce.2.cloned.1.call-update) | async-done | bytes 81936 | tf_op jit(solution)/shard_map/psum | solution.py:183
  168.8 0.9 slice_multiply_fusion.4
  169.7 0.1 multiply_subtract_fusion.23
  169.8 0.7 fusion.18
  170.5 0.2 copy-done.2
  170.7 0.7 copy.19
  (48 shorter events, 0.7 us)
Async XLA Ops:
  7.2 161.7 %all-reduce.2.cloned.1.call-start = ((), (), s32[]{:S(2)}) async-start(), calls=%async_computation | async-start | bytes 262144 | tf_op jit(solution)/shard_map/psum | solution.py:183
  9.1 6.0 %copy-start.6 = (s32[4096]{0:T(1024)S(1)}, s32[4096]{0:T(1024)}, u32[]{:S(2)}) copy-start(s32[4096]{0:T(1024)} %param.15) | copy-start | bytes 49156
  9.1 6.1 %copy-start = (f32[4,8,4096]{2,1,0:T(8,128)S(1)}, f32[4,8,4096]{2,1,0:T(8,128)}, u32[]{:S(2)}) copy-start(f32[4,8,4096]{2,1,0:T(8,128)} %param.11) | copy-start | bytes 1572868
  9.2 5.9 %copy-start.1 = (f32[3,4096]{1,0:T(4,128)S(1)}, f32[3,4096]{1,0:T(4,128)}, u32[]{:S(2)}) copy-start(f32[3,4096]{1,0:T(4,128)} %param.14) | copy-start | bytes 147460
  9.2 10.3 %collective-permute-start = (f32[4,8,1]{2,1,0:T(8,128)S(1)}, f32[4,8,1]{2,1,0:T(8,128)S(1)}, u32[]{:S(2)}, u32[]{:S(2)}) collective-permute-start(f32[4,8,1]{2,1,0:T(8,128)S(1)} %get-tuple-element.55), channel_id=1, source_target_pairs={{0,1},{1,2},{2,3},{3,4},{4,5},{5,6},{6,7},{7,8},{8,9},{9,10},{10,1... | collective-permute-start | bytes 392 | tf_op jit(solution)/shard_map/ppermute | solution.py:20
  13.7 5.8 %collective-permute-start.1 = (f32[4,8,1]{2,1,0:T(8,128)S(1)}, f32[4,8,1]{2,1,0:T(8,128)S(1)}, u32[]{:S(2)}, u32[]{:S(2)}) collective-permute-start(f32[4,8,1]{2,1,0:T(8,128)S(1)} %get-tuple-element.54), channel_id=1, source_target_pairs={{1,0},{2,1},{3,2},{4,3},{5,4},{6,5},{7,6},{8,7},{9,8},{10,9},{11,1... | collective-permute-start | bytes 392 | tf_op jit(solution)/shard_map/ppermute | solution.py:22
  15.4 0.7 copy-start.13
  15.4 0.7 copy-start.14
  16.3 0.7 copy-start.10
  17.1 0.7 copy-start.9
  20.0 0.7 copy-start.3
  21.9 8.1 %collective-permute-start.2 = (f32[4,8,1]{2,1,0:T(8,128)}, f32[4,8,1]{2,1,0:T(8,128)}, u32[]{:S(2)}, u32[]{:S(2)}) collective-permute-start(f32[4,8,1]{2,1,0:T(8,128)} %get-tuple-element.50), channel_id=1, source_target_pairs={{0,1},{1,2},{2,3},{3,4},{4,5},{5,6},{6,7},{7,8},{8,9},{9,10},{10,1... | collective-permute-start | bytes 392 | tf_op jit(solution)/shard_map/ppermute | solution.py:20
  26.6 4.8 %collective-permute-start.3 = (f32[4,8,1]{2,1,0:T(8,128)}, f32[4,8,1]{2,1,0:T(8,128)}, u32[]{:S(2)}, u32[]{:S(2)}) collective-permute-start(f32[4,8,1]{2,1,0:T(8,128)} %get-tuple-element.51), channel_id=1, source_target_pairs={{1,0},{2,1},{3,2},{4,3},{5,4},{6,5},{7,6},{8,7},{9,8},{10,9},{11,1... | collective-permute-start | bytes 392 | tf_op jit(solution)/shard_map/ppermute | solution.py:22
  27.9 0.7 copy-start.12
  28.6 0.7 copy-start.11
  32.6 0.7 copy-start.4
  32.6 0.7 copy-start.7
  33.7 5.8 %collective-permute-start.4 = (f32[4,8,1]{2,1,0:T(8,128)S(1)}, f32[4,8,1]{2,1,0:T(8,128)S(1)}, u32[]{:S(2)}, u32[]{:S(2)}) collective-permute-start(f32[4,8,1]{2,1,0:T(8,128)S(1)} %get-tuple-element.46), channel_id=1, source_target_pairs={{0,1},{1,2},{2,3},{3,4},{4,5},{5,6},{6,7},{7,8},{8,9},{9,10},{10,1... | collective-permute-start | bytes 392 | tf_op jit(solution)/shard_map/ppermute | solution.py:20
  38.1 5.7 %collective-permute-start.5 = (f32[4,8,1]{2,1,0:T(8,128)S(1)}, f32[4,8,1]{2,1,0:T(8,128)S(1)}, u32[]{:S(2)}, u32[]{:S(2)}) collective-permute-start(f32[4,8,1]{2,1,0:T(8,128)S(1)} %get-tuple-element.47), channel_id=1, source_target_pairs={{1,0},{2,1},{3,2},{4,3},{5,4},{6,5},{7,6},{8,7},{9,8},{10,9},{11,1... | collective-permute-start | bytes 392 | tf_op jit(solution)/shard_map/ppermute | solution.py:22
  44.7 6.0 %collective-permute-start.6 = (f32[4,8,1]{2,1,0:T(8,128)S(1)}, f32[4,8,1]{2,1,0:T(8,128)S(1)}, u32[]{:S(2)}, u32[]{:S(2)}) collective-permute-start(f32[4,8,1]{2,1,0:T(8,128)S(1)} %get-tuple-element.42), channel_id=1, source_target_pairs={{0,1},{1,2},{2,3},{3,4},{4,5},{5,6},{6,7},{7,8},{8,9},{9,10},{10,1... | collective-permute-start | bytes 392 | tf_op jit(solution)/shard_map/ppermute | solution.py:20
  49.3 4.5 %collective-permute-start.7 = (f32[4,8,1]{2,1,0:T(8,128)S(1)}, f32[4,8,1]{2,1,0:T(8,128)S(1)}, u32[]{:S(2)}, u32[]{:S(2)}) collective-permute-start(f32[4,8,1]{2,1,0:T(8,128)S(1)} %get-tuple-element.43), channel_id=1, source_target_pairs={{1,0},{2,1},{3,2},{4,3},{5,4},{6,5},{7,6},{8,7},{9,8},{10,9},{11,1... | collective-permute-start | bytes 392 | tf_op jit(solution)/shard_map/ppermute | solution.py:22
  54.2 0.7 copy-start.8
  55.1 114.8 %copy-start.5 = (f32[4096]{0:T(1024)S(1)}, f32[4096]{0:T(1024)}, u32[]{:S(2)}) copy-start(f32[4096]{0:T(1024)} %convert_element_type.10) | copy-start | bytes 49156
  169.8 0.9 copy-start.2
Sparse Core Ops, SparseCore 0:
  30.1 138.6 all-reduce.1
where the time goes:
time: 179 us; the launch traced here: 178 us
  waiting for transfers between devices  122 us (68%)
  starting transfers between devices  23.4 us (13%)
  between operations  14.6 us (8%)
  other arithmetic  11.3 us (6%)
  local copies, waits for them, and re-layouts  7.48 us (4%)
    psum x1, waiting for transfers between devices, local(): totals = lax.psum(partial_value, 'modes')  113 us
    ppermute x4, starting transfers between devices, extended(): lax.ppermute(tail, axis, [(i, (i + 1) % count) for i in range(ends)])  18.2 us
    ppermute x4, waiting for transfers between devices, extended(): lax.ppermute(head, axis, [((i + 1) % count, i) for i in range(ends)])  8.79 us
    unnamed x31, local copies, waits for them, and re-layouts  5.75 us
    ppermute x4, starting transfers between devices, extended(): lax.ppermute(head, axis, [((i + 1) % count, i) for i in range(ends)])  5.16 us
  transfers between devices with their start and end apart: 9, of which 4 were waited for; matrix products, arithmetic and copies ran while one was open for 4% of the time, Pallas kernels for 0%

commit v1 on v0

--- a/solution.py
+++ b/solution.py
@@ -180,7 +180,7 @@
     partial_value = (
         densities_of(wave_state, right_w, cosine, sine_term, mode_weight) * row_scale[:, None]
     )
-    totals = lax.psum(partial_value, "modes")
+    totals = jnp.sum(lax.all_gather(partial_value, "modes"), axis=0)
     magnet_next = advance(magnet, mask_float, totals)
     return (next_state, totals, magnet_next)
 

time: 179 us -> 86.9 us (0.49)
  waiting for transfers between devices: 122 us -> 34.3 us
  local copies, waits for them, and re-layouts: 7.48 us -> 2.37 us
    psum x1 -> x0, waiting for transfers between devices: 113 us -> none  [local(): totals = lax.psum(partial_value, 'modes')]
    all_gather x0 -> x1, waiting for transfers between devices: none -> 24.1 us  [local(): totals = jnp.sum(lax.all_gather(partial_value, 'modes'), axis=0)]
    unnamed x31 -> x30, local copies, waits for them, and re-layouts: 5.75 us -> 0.59 us
  transfers between devices with their start and end apart: 9 -> 9, of which waited for: 4 -> 5; matrix products, arithmetic and copies ran while one was open for 4% -> 9% of each run, Pallas kernels for 0% -> 0%
where the time goes in v1:
time: 86.9 us; the launch traced here: 86.3 us
  waiting for transfers between devices  34.3 us (39%)
  starting transfers between devices  22.8 us (26%)
  between operations  14.7 us (17%)
  other arithmetic  12.1 us (14%)
  local copies, waits for them, and re-layouts  2.37 us (3%)
    all_gather x1, waiting for transfers between devices, local(): totals = jnp.sum(lax.all_gather(partial_value, 'modes'), axis=0)  24.1 us
    ppermute x4, starting transfers between devices, extended(): lax.ppermute(tail, axis, [(i, (i + 1) % count) for i in range(ends)])  17.6 us
    ppermute x4, waiting for transfers between devices, extended(): lax.ppermute(head, axis, [((i + 1) % count, i) for i in range(ends)])  10.2 us
    ppermute x4, starting transfers between devices, extended(): lax.ppermute(head, axis, [((i + 1) % count, i) for i in range(ends)])  5.16 us
    add x3, other arithmetic, rate(): left_w + right_w  1.75 us
    reduce_sum x1, other arithmetic, local(): totals = jnp.sum(lax.all_gather(partial_value, 'modes'), axis=0)  1.74 us
  transfers between devices with their start and end apart: 9, of which 5 were waited for; matrix products, arithmetic and copies ran while one was open for 9% of the time, Pallas kernels for 0%

profile of v1, /device:TPU:1, one launch (start us, length us, event | category | flops | bytes accessed | tf_op | source)
XLA Modules:
  0.0 86.3 jit_solution(18144337857274606931)
XLA Ops:
  7.2 0.0 all-gather.2.cloned.1.call-start
  7.2 0.8 fusion.28
  8.1 1.1 %multiply_add_fusion.13 = (f32[2,1,8,4096]{3,2,1,0:T(8,128)S(1)}, f32[2,1,8,4096]{3,2,1,0:T(8,128)S(1)}) fusion(f32[2,2,8,4096]{3,2,1,0:T(8,128)} %bitcast.27, f32[4096]{0:T(1024)S(1)} %get-tuple-element.65, f32[4096]{0:T(1024)S(1)} %get-tuple-element.64), kind=kLoop, calls=%fused_computation.64 | loop fusion | flops 393216 | bytes 1081344 | tf_op jit(solution)/shard_map/add | solution.py:34
  9.2 0.0 copy-start.13
  9.2 0.0 copy-start.10
  9.3 0.1 fusion.26
  9.3 4.4 %collective-permute-start = (f32[4,8,1]{2,1,0:T(8,128)S(1)}, f32[4,8,1]{2,1,0:T(8,128)S(1)}, u32[]{:S(2)}, u32[]{:S(2)}) collective-permute-start(f32[4,8,1]{2,1,0:T(8,128)S(1)} %get-tuple-element.55), channel_id=1, source_target_pairs={{0,1},{1,2},{2,3},{3,4},{4,5},{5,6},{6,7},{7,8},{8,9},{9,10},{10,1... | collective-permute-start | bytes 392 | tf_op jit(solution)/shard_map/ppermute | solution.py:20
  13.7 1.3 %collective-permute-start.1 = (f32[4,8,1]{2,1,0:T(8,128)S(1)}, f32[4,8,1]{2,1,0:T(8,128)S(1)}, u32[]{:S(2)}, u32[]{:S(2)}) collective-permute-start(f32[4,8,1]{2,1,0:T(8,128)S(1)} %get-tuple-element.54), channel_id=1, source_target_pairs={{1,0},{2,1},{3,2},{4,3},{5,4},{6,5},{7,6},{8,7},{9,8},{10,9},{11,1... | collective-permute-start | bytes 392 | tf_op jit(solution)/shard_map/ppermute | solution.py:22
  15.1 0.1 multiply_add_fusion.17
  15.4 0.2 select_reduce_fusion
  15.6 0.1 multiply_cosine_fusion
  15.7 0.1 and_convert_fusion
  15.8 0.6 pad_maximum_fusion.20
  16.4 0.6 pad_maximum_fusion.22
  17.0 0.6 convert_element_type.10
  17.6 0.8 collective-permute-done.1
  18.4 0.3 pad_maximum_fusion.6
  18.7 0.0 copy-start.3
  18.7 0.1 multiply_subtract_fusion
  18.9 0.1 pad_maximum_fusion.9
  18.9 0.5 copy-done.3
  19.4 0.1 fusion.5
  19.6 0.1 multiply_add_fusion.4
  19.7 0.0 copy-start.12
  19.7 0.1 multiply_add_fusion.16
  19.8 0.0 copy-start.11
  19.8 0.1 multiply_add_fusion.11
  19.9 0.7 fusion.24
  20.6 4.1 %collective-permute-start.2 = (f32[4,8,1]{2,1,0:T(8,128)}, f32[4,8,1]{2,1,0:T(8,128)}, u32[]{:S(2)}, u32[]{:S(2)}) collective-permute-start(f32[4,8,1]{2,1,0:T(8,128)} %get-tuple-element.50), channel_id=1, source_target_pairs={{0,1},{1,2},{2,3},{3,4},{4,5},{5,6},{6,7},{7,8},{8,9},{9,10},{10,1... | collective-permute-start | bytes 392 | tf_op jit(solution)/shard_map/ppermute | solution.py:20
  24.7 1.3 %collective-permute-start.3 = (f32[4,8,1]{2,1,0:T(8,128)}, f32[4,8,1]{2,1,0:T(8,128)}, u32[]{:S(2)}, u32[]{:S(2)}) collective-permute-start(f32[4,8,1]{2,1,0:T(8,128)} %get-tuple-element.51), channel_id=1, source_target_pairs={{1,0},{2,1},{3,2},{4,3},{5,4},{6,5},{7,6},{8,7},{9,8},{10,9},{11,1... | collective-permute-start | bytes 392 | tf_op jit(solution)/shard_map/ppermute | solution.py:22
  26.0 0.1 fusion.14
  26.1 0.3 multiply_reduce_fusion
  26.4 0.0 copy-start.4
  26.4 0.7 bitcast_multiply_fusion
  27.1 0.0 all-gather.2.cloned.1.call-update
  27.2 3.2 %collective-permute-done.3 = f32[4,8,1]{2,1,0:T(8,128)} collective-permute-done((f32[4,8,1]{2,1,0:T(8,128)}, f32[4,8,1]{2,1,0:T(8,128)}, u32[]{:S(2)}, u32[]{:S(2)}) %collective-permute-start.3) | collective-permute-done | bytes 160 | tf_op jit(solution)/shard_map/ppermute | solution.py:22
  30.4 1.1 %fusion.2 = f32[4,8,4096]{2,1,0:T(8,128)S(1)} fusion(f32[4,8,1]{2,1,0:T(8,128)} %collective-permute-done.3, f32[4,8,4096]{2,1,0:T(8,128)S(1)} %bitcast.34, f32[4,8,1]{2,1,0:T(8,128)} %collective-permute-done.2), kind=kLoop, calls=%fused_computation.10 | loop fusion | flops 393216 | bytes 1048832 | tf_op jit(solution)/shard_map/add | solution.py:75
  31.4 0.1 multiply_subtract_fusion.5
  31.6 0.1 multiply_add_fusion.1
  31.8 0.1 multiply_add_fusion.3
  31.8 0.1 multiply_add_fusion.9
  32.0 0.1 fusion.22
  32.0 4.6 %collective-permute-start.4 = (f32[4,8,1]{2,1,0:T(8,128)S(1)}, f32[4,8,1]{2,1,0:T(8,128)S(1)}, u32[]{:S(2)}, u32[]{:S(2)}) collective-permute-start(f32[4,8,1]{2,1,0:T(8,128)S(1)} %get-tuple-element.46), channel_id=1, source_target_pairs={{0,1},{1,2},{2,3},{3,4},{4,5},{5,6},{6,7},{7,8},{8,9},{9,10},{10,1... | collective-permute-start | bytes 392 | tf_op jit(solution)/shard_map/ppermute | solution.py:20
  36.6 1.3 %collective-permute-start.5 = (f32[4,8,1]{2,1,0:T(8,128)S(1)}, f32[4,8,1]{2,1,0:T(8,128)S(1)}, u32[]{:S(2)}, u32[]{:S(2)}) collective-permute-start(f32[4,8,1]{2,1,0:T(8,128)S(1)} %get-tuple-element.47), channel_id=1, source_target_pairs={{1,0},{2,1},{3,2},{4,3},{5,4},{6,5},{7,6},{8,7},{9,8},{10,9},{11,1... | collective-permute-start | bytes 392 | tf_op jit(solution)/shard_map/ppermute | solution.py:22
  37.9 0.1 multiply_add_fusion.15
  38.0 3.1 %collective-permute-done.5 = f32[4,8,1]{2,1,0:T(8,128)S(1)} collective-permute-done((f32[4,8,1]{2,1,0:T(8,128)S(1)}, f32[4,8,1]{2,1,0:T(8,128)S(1)}, u32[]{:S(2)}, u32[]{:S(2)}) %collective-permute-start.5) | collective-permute-done | bytes 160 | tf_op jit(solution)/shard_map/ppermute | solution.py:22
  41.1 0.3 fusion.1
  41.5 0.1 multiply_subtract_fusion.3
  41.6 0.1 multiply_add_fusion
  41.8 0.1 multiply_add_fusion.2
  41.8 0.1 multiply_add_fusion.7
  42.0 0.1 fusion.20
  42.0 4.6 %collective-permute-start.6 = (f32[4,8,1]{2,1,0:T(8,128)S(1)}, f32[4,8,1]{2,1,0:T(8,128)S(1)}, u32[]{:S(2)}, u32[]{:S(2)}) collective-permute-start(f32[4,8,1]{2,1,0:T(8,128)S(1)} %get-tuple-element.42), channel_id=1, source_target_pairs={{0,1},{1,2},{2,3},{3,4},{4,5},{5,6},{6,7},{7,8},{8,9},{9,10},{10,1... | collective-permute-start | bytes 392 | tf_op jit(solution)/shard_map/ppermute | solution.py:20
  46.6 1.3 %collective-permute-start.7 = (f32[4,8,1]{2,1,0:T(8,128)S(1)}, f32[4,8,1]{2,1,0:T(8,128)S(1)}, u32[]{:S(2)}, u32[]{:S(2)}) collective-permute-start(f32[4,8,1]{2,1,0:T(8,128)S(1)} %get-tuple-element.43), channel_id=1, source_target_pairs={{1,0},{2,1},{3,2},{4,3},{5,4},{6,5},{7,6},{8,7},{9,8},{10,9},{11,1... | collective-permute-start | bytes 392 | tf_op jit(solution)/shard_map/ppermute | solution.py:22
  47.9 0.1 multiply_add_fusion.14
  48.0 3.1 %collective-permute-done.7 = f32[4,8,1]{2,1,0:T(8,128)S(1)} collective-permute-done((f32[4,8,1]{2,1,0:T(8,128)S(1)}, f32[4,8,1]{2,1,0:T(8,128)S(1)}, u32[]{:S(2)}, u32[]{:S(2)}) %collective-permute-start.7) | collective-permute-done | bytes 160 | tf_op jit(solution)/shard_map/ppermute | solution.py:22
  51.1 0.3 fusion
  51.4 0.1 multiply_subtract_fusion.1
  51.6 0.1 fusion.9
  51.8 1.0 %fusion.11 = f32[4,8,4096]{2,1,0:T(8,128)} fusion(f32[4,8,4096]{2,1,0:T(8,128)S(1)} %copy-done, f32[2,8,4096]{2,1,0:T(8,128)S(1)} %get-tuple-element.41, f32[2,8,4096]{2,1,0:T(8,128)S(1)} %get-tuple-element.40, f32[2,8,4096]{2,1,0:T(8,128)S(1)} %get-tuple-element.45, f32[2,8,4096]{2,1,0:T(8,128)S(1)} %get-tuple-element.44, ...), kind=kLoop, calls=%fused_computation.38 | loop fusion | flops 1441792 | bytes 3145728 | tf_op jit(solution)/shard_map/add | solution.py:172
  52.8 24.1 %all-gather.2.cloned.1.call-done = f32[16,5,4096]{2,1,0:T(8,128)} async-done(((f32[1,5,4096]{2,1,0:T(8,128)}), f32[16,5,4096]{2,1,0:T(8,128)}) %all-gather.2.cloned.1.call-update) | async-done | bytes 1310736 | tf_op jit(solution)/shard_map/all_gather | solution.py:183
  76.9 1.7 %reduce_sum.32 = f32[5,4096]{1,0:T(8,128)S(1)} reduce(f32[16,5,4096]{2,1,0:T(8,128)} %all-gather.2.cloned.1.call-done, f32[]{:T(128)} %constant.14.clone.1), dimensions={0}, to_apply=%region_2.3 | reduce | flops 307200 | bytes 1392644 | tf_op jit(solution)/shard_map/reduce_sum | solution.py:183
  78.7 0.1 multiply_subtract_fusion.23
  78.8 0.7 fusion.18
  (48 shorter events, 0.7 us)
Async XLA Ops:
  7.2 8.0 %copy-start = (f32[4,8,4096]{2,1,0:T(8,128)S(1)}, f32[4,8,4096]{2,1,0:T(8,128)}, u32[]{:S(2)}) copy-start(f32[4,8,4096]{2,1,0:T(8,128)} %param.11) | copy-start | bytes 1572868
  7.2 7.8 %copy-start.6 = (s32[4096]{0:T(1024)S(1)}, s32[4096]{0:T(1024)}, u32[]{:S(2)}) copy-start(s32[4096]{0:T(1024)} %param.15) | copy-start | bytes 49156
  7.2 7.9 %copy-start.1 = (f32[3,4096]{1,0:T(4,128)S(1)}, f32[3,4096]{1,0:T(4,128)}, u32[]{:S(2)}) copy-start(f32[3,4096]{1,0:T(4,128)} %param.14) | copy-start | bytes 147460
  7.2 69.7 %all-gather.2.cloned.1.call-start = ((), (), s32[]{:S(2)}) async-start(), calls=%async_computation | async-start | bytes 2228224 | tf_op jit(solution)/shard_map/all_gather | solution.py:183
  9.2 6.2 %copy-start.13 = (f32[8]{0:T(128)S(1)}, f32[8]{0:T(128)}, u32[]{:S(2)}) copy-start(f32[8]{0:T(128)} %param.19) | copy-start | bytes 100
  9.2 6.2 %copy-start.14 = (s32[8]{0:T(128)S(1)}, s32[8]{0:T(128)}, u32[]{:S(2)}) copy-start(s32[8]{0:T(128)} %param.18) | copy-start | bytes 100
  9.2 6.5 %copy-start.10 = (s32[8]{0:T(128)S(1)}, s32[8]{0:T(128)}, u32[]{:S(2)}) copy-start(s32[8]{0:T(128)} %param.20) | copy-start | bytes 100
  9.3 6.5 %copy-start.9 = (f32[4,8]{1,0:T(4,128)S(1)}, f32[4,8]{1,0:T(4,128)}, u32[]{:S(2)}) copy-start(f32[4,8]{1,0:T(4,128)} %param.17) | copy-start | bytes 388
  9.3 8.3 %collective-permute-start = (f32[4,8,1]{2,1,0:T(8,128)S(1)}, f32[4,8,1]{2,1,0:T(8,128)S(1)}, u32[]{:S(2)}, u32[]{:S(2)}) collective-permute-start(f32[4,8,1]{2,1,0:T(8,128)S(1)} %get-tuple-element.55), channel_id=1, source_target_pairs={{0,1},{1,2},{2,3},{3,4},{4,5},{5,6},{6,7},{7,8},{8,9},{9,10},{10,1... | collective-permute-start | bytes 392 | tf_op jit(solution)/shard_map/ppermute | solution.py:20
  13.7 4.7 %collective-permute-start.1 = (f32[4,8,1]{2,1,0:T(8,128)S(1)}, f32[4,8,1]{2,1,0:T(8,128)S(1)}, u32[]{:S(2)}, u32[]{:S(2)}) collective-permute-start(f32[4,8,1]{2,1,0:T(8,128)S(1)} %get-tuple-element.54), channel_id=1, source_target_pairs={{1,0},{2,1},{3,2},{4,3},{5,4},{6,5},{7,6},{8,7},{9,8},{10,9},{11,1... | collective-permute-start | bytes 392 | tf_op jit(solution)/shard_map/ppermute | solution.py:22
  18.7 0.7 copy-start.3
  19.7 6.4 %copy-start.12 = (f32[8]{0:T(128)S(1)}, f32[8]{0:T(128)}, u32[]{:S(2)}) copy-start(f32[8]{0:T(128)} %param.16) | copy-start | bytes 100
  19.8 6.6 %copy-start.11 = (f32[5]{0:T(128)S(1)}, f32[5]{0:T(128)}, u32[]{:S(2)}) copy-start(f32[5]{0:T(128)} %constant.9.clone) | copy-start | bytes 64
  20.6 6.5 %collective-permute-start.2 = (f32[4,8,1]{2,1,0:T(8,128)}, f32[4,8,1]{2,1,0:T(8,128)}, u32[]{:S(2)}, u32[]{:S(2)}) collective-permute-start(f32[4,8,1]{2,1,0:T(8,128)} %get-tuple-element.50), channel_id=1, source_target_pairs={{0,1},{1,2},{2,3},{3,4},{4,5},{5,6},{6,7},{7,8},{8,9},{9,10},{10,1... | collective-permute-start | bytes 392 | tf_op jit(solution)/shard_map/ppermute | solution.py:20
  24.7 5.6 %collective-permute-start.3 = (f32[4,8,1]{2,1,0:T(8,128)}, f32[4,8,1]{2,1,0:T(8,128)}, u32[]{:S(2)}, u32[]{:S(2)}) collective-permute-start(f32[4,8,1]{2,1,0:T(8,128)} %get-tuple-element.51), channel_id=1, source_target_pairs={{1,0},{2,1},{3,2},{4,3},{5,4},{6,5},{7,6},{8,7},{9,8},{10,9},{11,1... | collective-permute-start | bytes 392 | tf_op jit(solution)/shard_map/ppermute | solution.py:22
  26.4 5.2 %copy-start.4 = (f32[4096]{0:T(1024)S(1)}, f32[4096]{0:T(1024)}, u32[]{:S(2)}) copy-start(f32[4096]{0:T(1024)} %param.12) | copy-start | bytes 49156
  26.4 5.2 %copy-start.7 = (f32[4,8]{1,0:T(4,128)S(1)}, f32[4,8]{1,0:T(4,128)}, u32[]{:S(2)}) copy-start(f32[4,8]{1,0:T(4,128)} %get-tuple-element.85) | copy-start | bytes 388
  32.0 6.0 %collective-permute-start.4 = (f32[4,8,1]{2,1,0:T(8,128)S(1)}, f32[4,8,1]{2,1,0:T(8,128)S(1)}, u32[]{:S(2)}, u32[]{:S(2)}) collective-permute-start(f32[4,8,1]{2,1,0:T(8,128)S(1)} %get-tuple-element.46), channel_id=1, source_target_pairs={{0,1},{1,2},{2,3},{3,4},{4,5},{5,6},{6,7},{7,8},{8,9},{9,10},{10,1... | collective-permute-start | bytes 392 | tf_op jit(solution)/shard_map/ppermute | solution.py:20
  36.6 4.5 %collective-permute-start.5 = (f32[4,8,1]{2,1,0:T(8,128)S(1)}, f32[4,8,1]{2,1,0:T(8,128)S(1)}, u32[]{:S(2)}, u32[]{:S(2)}) collective-permute-start(f32[4,8,1]{2,1,0:T(8,128)S(1)} %get-tuple-element.47), channel_id=1, source_target_pairs={{1,0},{2,1},{3,2},{4,3},{5,4},{6,5},{7,6},{8,7},{9,8},{10,9},{11,1... | collective-permute-start | bytes 392 | tf_op jit(solution)/shard_map/ppermute | solution.py:22
  42.0 6.0 %collective-permute-start.6 = (f32[4,8,1]{2,1,0:T(8,128)S(1)}, f32[4,8,1]{2,1,0:T(8,128)S(1)}, u32[]{:S(2)}, u32[]{:S(2)}) collective-permute-start(f32[4,8,1]{2,1,0:T(8,128)S(1)} %get-tuple-element.42), channel_id=1, source_target_pairs={{0,1},{1,2},{2,3},{3,4},{4,5},{5,6},{6,7},{7,8},{8,9},{9,10},{10,1... | collective-permute-start | bytes 392 | tf_op jit(solution)/shard_map/ppermute | solution.py:20
  46.6 5.0 %copy-start.8 = (f32[4,8]{1,0:T(4,128)S(1)}, f32[4,8]{1,0:T(4,128)}, u32[]{:S(2)}) copy-start(f32[4,8]{1,0:T(4,128)} %pad_maximum_fusion.22) | copy-start | bytes 388
  46.6 4.5 %collective-permute-start.7 = (f32[4,8,1]{2,1,0:T(8,128)S(1)}, f32[4,8,1]{2,1,0:T(8,128)S(1)}, u32[]{:S(2)}, u32[]{:S(2)}) collective-permute-start(f32[4,8,1]{2,1,0:T(8,128)S(1)} %get-tuple-element.43), channel_id=1, source_target_pairs={{1,0},{2,1},{3,2},{4,3},{5,4},{6,5},{7,6},{8,7},{9,8},{10,9},{11,1... | collective-permute-start | bytes 392 | tf_op jit(solution)/shard_map/ppermute | solution.py:22
  51.8 27.0 %copy-start.5 = (f32[4096]{0:T(1024)S(1)}, f32[4096]{0:T(1024)}, u32[]{:S(2)}) copy-start(f32[4096]{0:T(1024)} %convert_element_type.10) | copy-start | bytes 49156
  78.6 0.8 copy-start.2
Sparse Core Ops, SparseCore 0:
  27.3 49.5 all-gather.1
